TPU v7x, 32 devices: a whole 2x2x4 slice. The times are simulated.
32 devices in a mesh: dp: 8 (over z, y), fsdp: 4 (over x, core).
Axes of the slice: x: 2, y: 2, z: 4, core: 2. Of those that a mesh axis runs over, the one named last changes fastest.
Arguments:
- decoder_in: bfloat16 [2, 32, 256, 768], P(None, ('dp', 'fsdp')), may hold values from -6 to 6
- memory: bfloat16 [2, 32, 128, 768], P(None, ('dp', 'fsdp')), may hold values from -6 to 6
- out_grad: bfloat16 [2, 32, 256, 768], P(None, ('dp', 'fsdp')), may hold values from -6 to 6
- lengths: int32 [2, 32], P(None, ('dp', 'fsdp')), may hold values from 32 to 256, as said below
- self_query: bfloat16 [768, 768], P(('dp', 'fsdp')), may hold values from -0.02734375 to 0.02734375
- self_key: bfloat16 [768, 768], P(('dp', 'fsdp')), may hold values from -0.21875 to 0.21875
- self_value: bfloat16 [768, 768], P(('dp', 'fsdp')), may hold values from -0.21875 to 0.21875
- self_out: bfloat16 [768, 768], P(('dp', 'fsdp')), may hold values from -1.75 to 1.75
- cross_query: bfloat16 [768, 768], P(('dp', 'fsdp')), may hold values from -0.02734375 to 0.02734375
- cross_key: bfloat16 [768, 768], P(('dp', 'fsdp')), may hold values from -0.21875 to 0.21875
- cross_value: bfloat16 [768, 768], P(('dp', 'fsdp')), may hold values from -0.21875 to 0.21875
- cross_out: bfloat16 [768, 768], P(('dp', 'fsdp')), may hold values from -3.5 to 3.5
- ff_in: bfloat16 [768, 3072], P(('dp', 'fsdp')), may hold values from -0.21875 to 0.21875
- ff_out: bfloat16 [3072, 768], P(('dp', 'fsdp')), may hold values from -0.109375 to 0.109375
- norm_self: bfloat16 [768], P(('dp', 'fsdp')), may hold values from 0.25 to 1.75
- norm_cross: bfloat16 [768], P(('dp', 'fsdp')), may hold values from 0.25 to 1.75
- norm_ff: bfloat16 [768], P(('dp', 'fsdp')), may hold values from 0.25 to 1.75
- bucket_bias_table: bfloat16 [32, 12], replicated, may hold values from -4 to 4
Outputs:
- layer_out: bfloat16 [2, 32, 256, 768], P(None, ('dp', 'fsdp'))
- input_grad: float32 [2, 32, 256, 768], P(None, ('dp', 'fsdp'))
- memory_grad: float32 [2, 32, 128, 768], P(None, ('dp', 'fsdp'))
- self_query_grad: float32 [768, 768], P(('dp', 'fsdp'))
- self_key_grad: float32 [768, 768], P(('dp', 'fsdp'))
- self_value_grad: float32 [768, 768], P(('dp', 'fsdp'))
- self_out_grad: float32 [768, 768], P(('dp', 'fsdp'))
- cross_query_grad: float32 [768, 768], P(('dp', 'fsdp'))
- cross_key_grad: float32 [768, 768], P(('dp', 'fsdp'))
- cross_value_grad: float32 [768, 768], P(('dp', 'fsdp'))
- cross_out_grad: float32 [768, 768], P(('dp', 'fsdp'))
- ff_in_grad: float32 [768, 3072], P(('dp', 'fsdp'))
- ff_out_grad: float32 [3072, 768], P(('dp', 'fsdp'))
- norm_self_grad: float32 [768], P(('dp', 'fsdp'))
- norm_cross_grad: float32 [768], P(('dp', 'fsdp'))
- norm_ff_grad: float32 [768], P(('dp', 'fsdp'))
- bias_table_grad: float32 [32, 12], replicated
Inputs may be any that keep to these rules, and one draw needn't show every extreme that they name: `lengths`: every sequence has 32 to 256 tokens; some sequence of the batch has exactly 256.
All inputs are finite; a program needn't handle non-finite values.
Results may differ from a plain program's by a relative error of at most 0.019.
Values may be sent and summed in bfloat16 or wider, within the bound.
A program may use at most 320 MiB of HBM per device.

v0:
```python
import math

import jax
import jax.numpy as jnp
from jax import lax
from jax.sharding import PartitionSpec as P

HEADS = 12
BUCKETS = 32
MAX_DIST = 128


EPS = 1e-06
MASKED = -1e30
TOP_PRECISION = lax.Precision.HIGHEST


def bucket_onehot(length):
    half_count = BUCKETS // 2
    positions = jnp.arange(length, dtype=jnp.int32)
    distance = jnp.maximum(positions[:, None] - positions[None, :], 0)
    farther = jnp.zeros_like(distance)
    for level in range(1, half_count):
        border = int(math.ceil(half_count * (MAX_DIST / half_count) ** (level / half_count)))
        farther = farther + (distance >= border).astype(jnp.int32)
    bucket = jnp.where(distance < half_count, distance, half_count + farther)
    return (bucket[None] == jnp.arange(BUCKETS, dtype=jnp.int32)[:, None, None]).astype(jnp.float32)


def normalize(vector, gain_row):
    return vector * lax.rsqrt(jnp.mean(vector * vector, axis=-1, keepdims=True) + EPS) * gain_row


def project(operand, weight):
    return jnp.dot(operand, weight, preferred_element_type=jnp.float32)


def project_back(operand, weight):
    return lax.dot_general(
        operand, weight, (((1,), (1,)), ((), ())), preferred_element_type=jnp.float32
    )


def weight_grad(inputs_rows, grad_rows):
    return lax.dot_general(
        inputs_rows, grad_rows, (((0,), (0,)), ((), ())), preferred_element_type=jnp.float32
    )


def split_heads(matrix):
    return matrix.reshape(matrix.shape[0], HEADS, matrix.shape[1] // HEADS)


def head_scores(queries, key_rows):
    return jnp.einsum(
        "qhe,khe->hqk",
        split_heads(queries),
        split_heads(key_rows),
        preferred_element_type=jnp.float32,
    )


def attend_forward(queries, key_rows, values, relative_position_bias, allowed):
    scores = jnp.where(allowed, head_scores(queries, key_rows) + relative_position_bias, MASKED)
    largest = jnp.max(scores, axis=-1, keepdims=True)
    exponent = jnp.exp(scores - largest)
    row_totals = jnp.sum(exponent, axis=-1, keepdims=True)
    attention_weights = (exponent / row_totals).astype(jnp.bfloat16)
    context = jnp.einsum(
        "hqk,khe->qhe", attention_weights, split_heads(values), preferred_element_type=jnp.float32
    )
    return (context.reshape(queries.shape).astype(jnp.bfloat16), largest + jnp.log(row_totals))


def attend_backward(
    queries, key_rows, values, relative_position_bias, allowed, log_totals, grad_context
):
    scores = jnp.where(allowed, head_scores(queries, key_rows) + relative_position_bias, MASKED)
    attention_weights = jnp.exp(scores - log_totals)
    grad_heads = split_heads(grad_context)
    grad_values = jnp.einsum(
        "hqk,qhe->khe",
        attention_weights.astype(jnp.bfloat16),
        grad_heads,
        preferred_element_type=jnp.float32,
    )
    grad_weights = jnp.einsum(
        "qhe,khe->hqk", grad_heads, split_heads(values), preferred_element_type=jnp.float32
    )
    score_gradient = attention_weights * (
        grad_weights - jnp.sum(grad_weights * attention_weights, axis=-1, keepdims=True)
    )
    rounded = score_gradient.astype(jnp.bfloat16)
    grad_queries = jnp.einsum(
        "hqk,khe->qhe", rounded, split_heads(key_rows), preferred_element_type=jnp.float32
    )
    grad_keys = jnp.einsum(
        "hqk,qhe->khe", rounded, split_heads(queries), preferred_element_type=jnp.float32
    )
    return (
        grad_queries.reshape(queries.shape).astype(jnp.bfloat16),
        grad_keys.reshape(key_rows.shape).astype(jnp.bfloat16),
        grad_values.reshape(values.shape).astype(jnp.bfloat16),
        score_gradient,
    )


def masks_for(length_now, causal):
    positions = jnp.arange(causal.shape[0], dtype=jnp.int32)
    present = positions < length_now
    allowed = (causal & present[None, :])[None]
    return (present[:, None].astype(jnp.float32), allowed)


def forward_micro(decoded_bf, memory_bf, length_now, full, relative_position_bias, causal):
    (
        self_query,
        self_key,
        self_value,
        self_out,
        cross_query,
        cross_key,
        cross_value,
        cross_out,
        ff_in,
        ff_out,
        norm_self,
        norm_cross,
        norm_ff,
    ) = full
    valid_rows, allowed = masks_for(length_now, causal)
    decoded = decoded_bf.astype(jnp.float32)
    normed = normalize(decoded, norm_self.astype(jnp.float32)).astype(jnp.bfloat16)
    queries = project(normed, self_query).astype(jnp.bfloat16)
    key_rows = project(normed, self_key).astype(jnp.bfloat16)
    values = project(normed, self_value).astype(jnp.bfloat16)
    context, log_self = attend_forward(queries, key_rows, values, relative_position_bias, allowed)
    after_self = decoded + project(context, self_out)
    normed_cross = normalize(after_self, norm_cross.astype(jnp.float32)).astype(jnp.bfloat16)
    cross_queries = project(normed_cross, cross_query).astype(jnp.bfloat16)
    memory_keys = project(memory_bf, cross_key).astype(jnp.bfloat16)
    memory_values = project(memory_bf, cross_value).astype(jnp.bfloat16)
    cross_context, log_cross = attend_forward(cross_queries, memory_keys, memory_values, 0.0, True)
    after_cross = after_self + project(cross_context, cross_out)
    normed_ff = normalize(after_cross, norm_ff.astype(jnp.float32)).astype(jnp.bfloat16)
    hidden = project(normed_ff, ff_in)
    activated = jax.nn.gelu(hidden, approximate=True).astype(jnp.bfloat16)
    after_ff = after_cross + project(activated, ff_out)
    layer_rows = (after_ff * valid_rows).astype(jnp.bfloat16)
    kept = (
        decoded,
        normed,
        queries,
        key_rows,
        values,
        context,
        log_self,
        after_self,
        normed_cross,
        cross_queries,
        memory_keys,
        memory_values,
        cross_context,
        log_cross,
        after_cross,
        normed_ff,
        hidden,
        activated,
    )
    return (layer_rows, kept)


def backward_micro(
    kept, memory_bf, grad_bf, length_now, full, relative_position_bias, causal, bucket_indicator
):
    (
        self_query,
        self_key,
        self_value,
        self_out,
        cross_query,
        cross_key,
        cross_value,
        cross_out,
        ff_in,
        ff_out,
        norm_self,
        norm_cross,
        norm_ff,
    ) = full
    (
        decoded,
        normed,
        queries,
        key_rows,
        values,
        context,
        log_self,
        after_self,
        normed_cross,
        cross_queries,
        memory_keys,
        memory_values,
        cross_context,
        log_cross,
        after_cross,
        normed_ff,
        hidden,
        activated,
    ) = kept
    valid_rows, allowed = masks_for(length_now, causal)
    grad_after = grad_bf.astype(jnp.float32) * valid_rows
    grad_branch = grad_after.astype(jnp.bfloat16)
    grad_ff_out = weight_grad(activated, grad_branch)
    grad_activated = project_back(grad_branch, ff_out)
    gelu_pull = jax.vjp(lambda pre_act: jax.nn.gelu(pre_act, approximate=True), hidden)[1]
    grad_hidden = gelu_pull(grad_activated)[0].astype(jnp.bfloat16)
    grad_ff_in = weight_grad(normed_ff, grad_hidden)
    norm_pull = jax.vjp(normalize, after_cross, norm_ff.astype(jnp.float32))[1]
    grad_rows, grad_norm_ff = norm_pull(project_back(grad_hidden, ff_in))
    grad_after = grad_after + grad_rows
    grad_branch = grad_after.astype(jnp.bfloat16)
    grad_cross_out = weight_grad(cross_context, grad_branch)
    grad_context = project_back(grad_branch, cross_out).astype(jnp.bfloat16)
    grad_cross_rows, grad_memory_keys, grad_memory_values, unused = attend_backward(
        cross_queries, memory_keys, memory_values, 0.0, True, log_cross, grad_context
    )
    grad_cross_query = weight_grad(normed_cross, grad_cross_rows)
    grad_cross_key = weight_grad(memory_bf, grad_memory_keys)
    grad_cross_value = weight_grad(memory_bf, grad_memory_values)
    grad_memory = project_back(grad_memory_keys, cross_key) + project_back(
        grad_memory_values, cross_value
    )
    norm_pull = jax.vjp(normalize, after_self, norm_cross.astype(jnp.float32))[1]
    grad_rows, grad_norm_cross = norm_pull(project_back(grad_cross_rows, cross_query))
    grad_after = grad_after + grad_rows
    grad_branch = grad_after.astype(jnp.bfloat16)
    grad_self_out = weight_grad(context, grad_branch)
    grad_context = project_back(grad_branch, self_out).astype(jnp.bfloat16)
    grad_queries, grad_key_rows, grad_values, score_gradient = attend_backward(
        queries, key_rows, values, relative_position_bias, allowed, log_self, grad_context
    )
    grad_self_query = weight_grad(normed, grad_queries)
    grad_self_key = weight_grad(normed, grad_key_rows)
    grad_self_value = weight_grad(normed, grad_values)
    grad_normed = (
        project_back(grad_queries, self_query)
        + project_back(grad_key_rows, self_key)
        + project_back(grad_values, self_value)
    )
    norm_pull = jax.vjp(normalize, decoded, norm_self.astype(jnp.float32))[1]
    grad_rows, grad_norm_self = norm_pull(grad_normed)
    grad_input = grad_after + grad_rows
    relative_bias_gradient = jnp.einsum(
        "fgd,ogd->fo", bucket_indicator, score_gradient, precision=TOP_PRECISION
    )
    grads = (
        grad_self_query,
        grad_self_key,
        grad_self_value,
        grad_self_out,
        grad_cross_query,
        grad_cross_key,
        grad_cross_value,
        grad_cross_out,
        grad_ff_in,
        grad_ff_out,
        grad_norm_self,
        grad_norm_cross,
        grad_norm_ff,
    )
    return (grads, relative_bias_gradient, grad_input, grad_memory)


def body(
    decoder_in,
    memory,
    out_grad,
    lengths,
    self_query,
    self_key,
    self_value,
    self_out,
    cross_query,
    cross_key,
    cross_value,
    cross_out,
    ff_in,
    ff_out,
    norm_self,
    norm_cross,
    norm_ff,
    bucket_bias_table,
):
    shards = (
        self_query,
        self_key,
        self_value,
        self_out,
        cross_query,
        cross_key,
        cross_value,
        cross_out,
        ff_in,
        ff_out,
        norm_self,
        norm_cross,
        norm_ff,
    )
    seq_length = decoder_in.shape[2]
    bucket_indicator = bucket_onehot(seq_length)
    relative_position_bias = jnp.einsum(
        "fsn,fe->esn",
        bucket_indicator,
        bucket_bias_table.astype(jnp.float32),
        precision=TOP_PRECISION,
    )
    positions = jnp.arange(seq_length, dtype=jnp.int32)
    causal = positions[:, None] >= positions[None, :]
    devices = lax.axis_size(("dp", "fsdp"))

    def run_forward(carried, member):
        decoded_bf, memory_bf, length_now = member
        full = (
            lax.all_gather(self_query, ("dp", "fsdp"), axis=0, tiled=True),
            lax.all_gather(self_key, ("dp", "fsdp"), axis=0, tiled=True),
            lax.all_gather(self_value, ("dp", "fsdp"), axis=0, tiled=True),
            lax.all_gather(self_out, ("dp", "fsdp"), axis=0, tiled=True),
            lax.all_gather(cross_query, ("dp", "fsdp"), axis=0, tiled=True),
            lax.all_gather(cross_key, ("dp", "fsdp"), axis=0, tiled=True),
            lax.all_gather(cross_value, ("dp", "fsdp"), axis=0, tiled=True),
            lax.all_gather(cross_out, ("dp", "fsdp"), axis=0, tiled=True),
            lax.all_gather(ff_in, ("dp", "fsdp"), axis=0, tiled=True),
            lax.all_gather(ff_out, ("dp", "fsdp"), axis=0, tiled=True),
            lax.all_gather(norm_self, ("dp", "fsdp"), axis=0, tiled=True),
            lax.all_gather(norm_cross, ("dp", "fsdp"), axis=0, tiled=True),
            lax.all_gather(norm_ff, ("dp", "fsdp"), axis=0, tiled=True),
        )
        layer_rows, kept = forward_micro(
            decoded_bf, memory_bf, length_now, full, relative_position_bias, causal
        )
        return (carried, (layer_rows, kept))

    carried, (layer_out, kept_all) = lax.scan(
        run_forward, jnp.zeros((), jnp.int32), (decoder_in[:, 0], memory[:, 0], lengths[:, 0])
    )
    initial = tuple(
        (jnp.zeros((shard.shape[0] * devices,) + shard.shape[1:], jnp.float32) for shard in shards)
    ) + (
        jnp.zeros(bucket_bias_table.shape, jnp.float32),
    )

    def run_backward(running, member):
        kept, memory_bf, grad_bf, length_now = member
        full = (
            lax.all_gather(self_query, ("dp", "fsdp"), axis=0, tiled=True),
            lax.all_gather(self_key, ("dp", "fsdp"), axis=0, tiled=True),
            lax.all_gather(self_value, ("dp", "fsdp"), axis=0, tiled=True),
            lax.all_gather(self_out, ("dp", "fsdp"), axis=0, tiled=True),
            lax.all_gather(cross_query, ("dp", "fsdp"), axis=0, tiled=True),
            lax.all_gather(cross_key, ("dp", "fsdp"), axis=0, tiled=True),
            lax.all_gather(cross_value, ("dp", "fsdp"), axis=0, tiled=True),
            lax.all_gather(cross_out, ("dp", "fsdp"), axis=0, tiled=True),
            lax.all_gather(ff_in, ("dp", "fsdp"), axis=0, tiled=True),
            lax.all_gather(ff_out, ("dp", "fsdp"), axis=0, tiled=True),
            lax.all_gather(norm_self, ("dp", "fsdp"), axis=0, tiled=True),
            lax.all_gather(norm_cross, ("dp", "fsdp"), axis=0, tiled=True),
            lax.all_gather(norm_ff, ("dp", "fsdp"), axis=0, tiled=True),
        )
        grads, relative_bias_gradient, grad_input, grad_memory = backward_micro(
            kept,
            memory_bf,
            grad_bf,
            length_now,
            full,
            relative_position_bias,
            causal,
            bucket_indicator,
        )
        adding = grads + (relative_bias_gradient,)
        running = tuple((earlier + addend for earlier, addend in zip(running, adding)))
        return (running, (grad_input, grad_memory))

    running, (grad_inputs, grad_memories) = lax.scan(
        run_backward, initial, (kept_all, memory[:, 0], out_grad[:, 0], lengths[:, 0])
    )
    summed = (
        lax.psum_scatter(running[0], ("dp", "fsdp"), scatter_dimension=0, tiled=True),
        lax.psum_scatter(running[1], ("dp", "fsdp"), scatter_dimension=0, tiled=True),
        lax.psum_scatter(running[2], ("dp", "fsdp"), scatter_dimension=0, tiled=True),
        lax.psum_scatter(running[3], ("dp", "fsdp"), scatter_dimension=0, tiled=True),
        lax.psum_scatter(running[4], ("dp", "fsdp"), scatter_dimension=0, tiled=True),
        lax.psum_scatter(running[5], ("dp", "fsdp"), scatter_dimension=0, tiled=True),
        lax.psum_scatter(running[6], ("dp", "fsdp"), scatter_dimension=0, tiled=True),
        lax.psum_scatter(running[7], ("dp", "fsdp"), scatter_dimension=0, tiled=True),
        lax.psum_scatter(running[8], ("dp", "fsdp"), scatter_dimension=0, tiled=True),
        lax.psum_scatter(running[9], ("dp", "fsdp"), scatter_dimension=0, tiled=True),
        lax.psum_scatter(running[10], ("dp", "fsdp"), scatter_dimension=0, tiled=True),
        lax.psum_scatter(running[11], ("dp", "fsdp"), scatter_dimension=0, tiled=True),
        lax.psum_scatter(running[12], ("dp", "fsdp"), scatter_dimension=0, tiled=True),
    )
    pieces = tuple(summed) + (lax.psum(running[13], ("dp", "fsdp")),)
    bias_grad = pieces[13]
    return (
        layer_out[:, None],
        grad_inputs[:, None],
        grad_memories[:, None],
        pieces[0],
        pieces[1],
        pieces[2],
        pieces[3],
        pieces[4],
        pieces[5],
        pieces[6],
        pieces[7],
        pieces[8],
        pieces[9],
        pieces[10],
        pieces[11],
        pieces[12],
        bias_grad,
    )


def solution(mesh):
    return jax.shard_map(
        body,
        mesh=mesh,
        in_specs=(
            P(None, ("dp", "fsdp"), None, None),
            P(None, ("dp", "fsdp"), None, None),
            P(None, ("dp", "fsdp"), None, None),
            P(None, ("dp", "fsdp")),
            P(("dp", "fsdp"), None),
            P(("dp", "fsdp"), None),
            P(("dp", "fsdp"), None),
            P(("dp", "fsdp"), None),
            P(("dp", "fsdp"), None),
            P(("dp", "fsdp"), None),
            P(("dp", "fsdp"), None),
            P(("dp", "fsdp"), None),
            P(("dp", "fsdp"), None),
            P(("dp", "fsdp"), None),
            P(("dp", "fsdp")),
            P(("dp", "fsdp")),
            P(("dp", "fsdp")),
            P(),
        ),
        out_specs=(
            P(None, ("dp", "fsdp"), None, None),
            P(None, ("dp", "fsdp"), None, None),
            P(None, ("dp", "fsdp"), None, None),
            P(("dp", "fsdp"), None),
            P(("dp", "fsdp"), None),
            P(("dp", "fsdp"), None),
            P(("dp", "fsdp"), None),
            P(("dp", "fsdp"), None),
            P(("dp", "fsdp"), None),
            P(("dp", "fsdp"), None),
            P(("dp", "fsdp"), None),
            P(("dp", "fsdp"), None),
            P(("dp", "fsdp"), None),
            P(("dp", "fsdp")),
            P(("dp", "fsdp")),
            P(("dp", "fsdp")),
            P(),
        ),
        check_vma=False,
    )
```

profile of v0, /device:TPU:0, one launch (start us, length us, event | category | flops | bytes accessed | tf_op | source)
XLA Modules:
  0.0 3505.2 jit_solution(3258747190756008937)
XLA Ops:
  19.8 1173.0 %while.90 = (s32[]{:T(128)}, bf16[2,256,768]{2,1,0:T(8,128)(2,1)}, f32[2,256,768]{2,1,0:T(8,128)}, bf16[2,256,768]{2,1,0:T(8,128)(2,1)}, bf16[2,256,768]{2,1,0:T...) while((s32[]{:T(128)}, bf16[2,256,768]{2,1,0:T(8,128)(2,1)}, ...), condition=%wide.region_8.9_spmd.clone, body=%wide.region_0.8_spmd.clone.sunk | while | flops 4864409600 | bytes 228200976 | solution.py:344
  305.9 53.9 %all-gather.31.cloned.1.call-done = bf16[768,768]{1,0:T(8,128)(2,1)} async-done(((bf16[24,768]{1,0:T(8,128)(2,1)}), bf16[768,768]{1,0:T(8,128)(2,1)}) %all-gather.31.cloned.1.call-update) | async-done | bytes 1179664 | tf_op jit(solution)/shard_map/while/body/eval_jaxpr/all_gather | solution.py:329
  361.8 53.8 %all-gather.33.cloned.1.call-done = bf16[768,768]{1,0:T(8,128)(2,1)} async-done(((bf16[24,768]{1,0:T(8,128)(2,1)}), bf16[768,768]{1,0:T(8,128)(2,1)}) %all-gather.33.cloned.1.call-update) | async-done | bytes 1179664 | tf_op jit(solution)/shard_map/while/body/eval_jaxpr/all_gather | solution.py:330
  477.1 59.9 %all-gather.39.cloned.1.call-done = bf16[768,3072]{1,0:T(8,128)(2,1)} async-done(((bf16[24,3072]{1,0:T(8,128)(2,1)}), bf16[768,3072]{1,0:T(8,128)(2,1)}) %all-gather.39.cloned.1.call-update) | async-done | bytes 4718608 | tf_op jit(solution)/shard_map/while/body/eval_jaxpr/all_gather | solution.py:333
  546.3 56.0 %all-gather.37.cloned.1.call-done = bf16[3072,768]{1,0:T(8,128)(2,1)} async-done(((bf16[96,768]{1,0:T(8,128)(2,1)}), bf16[3072,768]{1,0:T(8,128)(2,1)}) %all-gather.37.cloned.1.call-update) | async-done | bytes 4718608 | tf_op jit(solution)/shard_map/while/body/eval_jaxpr/all_gather | solution.py:334
  890.4 53.9 %all-gather.31.cloned.1.call-done = bf16[768,768]{1,0:T(8,128)(2,1)} async-done(((bf16[24,768]{1,0:T(8,128)(2,1)}), bf16[768,768]{1,0:T(8,128)(2,1)}) %all-gather.31.cloned.1.call-update) | async-done | bytes 1179664 | tf_op jit(solution)/shard_map/while/body/eval_jaxpr/all_gather | solution.py:329
  946.3 53.7 %all-gather.33.cloned.1.call-done = bf16[768,768]{1,0:T(8,128)(2,1)} async-done(((bf16[24,768]{1,0:T(8,128)(2,1)}), bf16[768,768]{1,0:T(8,128)(2,1)}) %all-gather.33.cloned.1.call-update) | async-done | bytes 1179664 | tf_op jit(solution)/shard_map/while/body/eval_jaxpr/all_gather | solution.py:330
  1061.4 59.9 %all-gather.39.cloned.1.call-done = bf16[768,3072]{1,0:T(8,128)(2,1)} async-done(((bf16[24,3072]{1,0:T(8,128)(2,1)}), bf16[768,3072]{1,0:T(8,128)(2,1)}) %all-gather.39.cloned.1.call-update) | async-done | bytes 4718608 | tf_op jit(solution)/shard_map/while/body/eval_jaxpr/all_gather | solution.py:333
  1130.5 56.0 %all-gather.37.cloned.1.call-done = bf16[3072,768]{1,0:T(8,128)(2,1)} async-done(((bf16[96,768]{1,0:T(8,128)(2,1)}), bf16[3072,768]{1,0:T(8,128)(2,1)}) %all-gather.37.cloned.1.call-update) | async-done | bytes 4718608 | tf_op jit(solution)/shard_map/while/body/eval_jaxpr/all_gather | solution.py:334
  1194.0 1186.4 %while.91 = (s32[]{:T(128)}, f32[768,768]{1,0:T(8,128)}, f32[768,768]{1,0:T(8,128)}, f32[768,768]{1,0:T(8,128)}, f32[768,768]{1,0:T(8,128)}, /*index=5*/f32[768,...) while((s32[]{:T(128)}, f32[768,768]{1,0:T(8,128)}, ...), condition=%wide.region_21.22_spmd.clone, body=%wide.region_9.21_spmd.clone.sunk | while | flops 10178699264 | bytes 542102144 | solution.py:384
  1575.5 52.9 %all-gather.53.cloned.1.call-done = bf16[768,768]{1,0:T(8,128)(2,1)} async-done(((bf16[24,768]{1,0:T(8,128)(2,1)}), bf16[768,768]{1,0:T(8,128)(2,1)}) %all-gather.53.cloned.1.call-update) | async-done | bytes 1179664 | tf_op jit(solution)/shard_map/while/body/eval_jaxpr/all_gather | solution.py:357
  1631.4 52.9 %all-gather.55.cloned.1.call-done = bf16[768,768]{1,0:T(8,128)(2,1)} async-done(((bf16[24,768]{1,0:T(8,128)(2,1)}), bf16[768,768]{1,0:T(8,128)(2,1)}) %all-gather.55.cloned.1.call-update) | async-done | bytes 1179664 | tf_op jit(solution)/shard_map/while/body/eval_jaxpr/all_gather | solution.py:358
  2157.3 53.0 %all-gather.53.cloned.1.call-done = bf16[768,768]{1,0:T(8,128)(2,1)} async-done(((bf16[24,768]{1,0:T(8,128)(2,1)}), bf16[768,768]{1,0:T(8,128)(2,1)}) %all-gather.53.cloned.1.call-update) | async-done | bytes 1179664 | tf_op jit(solution)/shard_map/while/body/eval_jaxpr/all_gather | solution.py:357
  2213.2 52.9 %all-gather.55.cloned.1.call-done = bf16[768,768]{1,0:T(8,128)(2,1)} async-done(((bf16[24,768]{1,0:T(8,128)(2,1)}), bf16[768,768]{1,0:T(8,128)(2,1)}) %all-gather.55.cloned.1.call-update) | async-done | bytes 1179664 | tf_op jit(solution)/shard_map/while/body/eval_jaxpr/all_gather | solution.py:358
  2428.2 56.3 %reduce-scatter.11.cloned.1.call-done = f32[24,768]{1,0:T(8,128)} async-done(((f32[768,768]{1,0:T(8,128)}), f32[24,768]{1,0:T(8,128)}) %reduce-scatter.11.cloned.1.call-update) | async-done | bytes 73744 | tf_op jit(solution)/shard_map/reduce_scatter | solution.py:388
  2484.5 104.6 %reduce-scatter.13.cloned.1.call-done = f32[24,768]{1,0:T(8,128)} async-done(((f32[768,768]{1,0:T(8,128)}), f32[24,768]{1,0:T(8,128)}) %reduce-scatter.13.cloned.1.call-update) | async-done | bytes 73744 | tf_op jit(solution)/shard_map/reduce_scatter | solution.py:389
  2589.1 103.7 %reduce-scatter.15.cloned.1.call-done = f32[24,768]{1,0:T(8,128)} async-done(((f32[768,768]{1,0:T(8,128)}), f32[24,768]{1,0:T(8,128)}) %reduce-scatter.15.cloned.1.call-update) | async-done | bytes 73744 | tf_op jit(solution)/shard_map/reduce_scatter | solution.py:390
  2692.8 104.7 %reduce-scatter.17.cloned.1.call-done = f32[24,768]{1,0:T(8,128)} async-done(((f32[768,768]{1,0:T(8,128)}), f32[24,768]{1,0:T(8,128)}) %reduce-scatter.17.cloned.1.call-update) | async-done | bytes 73744 | tf_op jit(solution)/shard_map/reduce_scatter | solution.py:391
  2797.5 103.8 %reduce-scatter.19.cloned.1.call-done = f32[24,768]{1,0:T(8,128)} async-done(((f32[768,768]{1,0:T(8,128)}), f32[24,768]{1,0:T(8,128)}) %reduce-scatter.19.cloned.1.call-update) | async-done | bytes 73744 | tf_op jit(solution)/shard_map/reduce_scatter | solution.py:392
  2901.3 104.6 %reduce-scatter.21.cloned.1.call-done = f32[24,768]{1,0:T(8,128)} async-done(((f32[768,768]{1,0:T(8,128)}), f32[24,768]{1,0:T(8,128)}) %reduce-scatter.21.cloned.1.call-update) | async-done | bytes 73744 | tf_op jit(solution)/shard_map/reduce_scatter | solution.py:393
  3006.0 103.7 %reduce-scatter.23.cloned.1.call-done = f32[24,768]{1,0:T(8,128)} async-done(((f32[768,768]{1,0:T(8,128)}), f32[24,768]{1,0:T(8,128)}) %reduce-scatter.23.cloned.1.call-update) | async-done | bytes 73744 | tf_op jit(solution)/shard_map/reduce_scatter | solution.py:394
  3109.7 104.5 %reduce-scatter.25.cloned.1.call-done = f32[24,768]{1,0:T(8,128)} async-done(((f32[768,768]{1,0:T(8,128)}), f32[24,768]{1,0:T(8,128)}) %reduce-scatter.25.cloned.1.call-update) | async-done | bytes 73744 | tf_op jit(solution)/shard_map/reduce_scatter | solution.py:395
  3214.3 141.0 %reduce-scatter.27.cloned.1.call-done = f32[24,3072]{1,0:T(8,128)} async-done(((f32[768,3072]{1,0:T(8,128)}), f32[24,3072]{1,0:T(8,128)}) %reduce-scatter.27.cloned.1.call-update) | async-done | bytes 294928 | tf_op jit(solution)/shard_map/reduce_scatter | solution.py:396
  3355.3 142.1 %reduce-scatter.29.cloned.1.call-done = f32[96,768]{1,0:T(8,128)} async-done(((f32[3072,768]{1,0:T(8,128)}), f32[96,768]{1,0:T(8,128)}) %reduce-scatter.29.cloned.1.call-update) | async-done | bytes 294928 | tf_op jit(solution)/shard_map/reduce_scatter | solution.py:397
  (849 shorter events, 1734.3 us)
Async XLA Ops:
  24.1 391.6 %all-gather.33.cloned.1.call-start = ((), (), s32[]{:S(2)}) async-start(), calls=%async_computation.26 | async-start | bytes 1216512 | tf_op jit(solution)/shard_map/while/body/eval_jaxpr/all_gather | solution.py:330
  24.8 446.7 %all-gather.35.cloned.1.call-start = ((), (), s32[]{:S(2)}) async-start(), calls=%async_computation.27 | async-start | bytes 1216512 | tf_op jit(solution)/shard_map/while/body/eval_jaxpr/all_gather | solution.py:332
  25.6 511.5 %all-gather.39.cloned.1.call-start = ((), (), s32[]{:S(2)}) async-start(), calls=%async_computation.29 | async-start | bytes 4866048 | tf_op jit(solution)/shard_map/while/body/eval_jaxpr/all_gather | solution.py:333
  26.3 576.0 %all-gather.37.cloned.1.call-start = ((), (), s32[]{:S(2)}) async-start(), calls=%async_computation.28 | async-start | bytes 4866048 | tf_op jit(solution)/shard_map/while/body/eval_jaxpr/all_gather | solution.py:334
  612.4 387.6 %all-gather.33.cloned.1.call-start = ((), (), s32[]{:S(2)}) async-start(), calls=%async_computation.26 | async-start | bytes 1216512 | tf_op jit(solution)/shard_map/while/body/eval_jaxpr/all_gather | solution.py:330
  613.0 442.8 %all-gather.35.cloned.1.call-start = ((), (), s32[]{:S(2)}) async-start(), calls=%async_computation.27 | async-start | bytes 1216512 | tf_op jit(solution)/shard_map/while/body/eval_jaxpr/all_gather | solution.py:332
  613.5 507.7 %all-gather.39.cloned.1.call-start = ((), (), s32[]{:S(2)}) async-start(), calls=%async_computation.29 | async-start | bytes 4866048 | tf_op jit(solution)/shard_map/while/body/eval_jaxpr/all_gather | solution.py:333
  614.3 572.2 %all-gather.37.cloned.1.call-start = ((), (), s32[]{:S(2)}) async-start(), calls=%async_computation.28 | async-start | bytes 4866048 | tf_op jit(solution)/shard_map/while/body/eval_jaxpr/all_gather | solution.py:334
  1221.7 406.7 %all-gather.53.cloned.1.call-start = ((), (), s32[]{:S(2)}) async-start(), calls=%async_computation.36 | async-start | bytes 1216512 | tf_op jit(solution)/shard_map/while/body/eval_jaxpr/all_gather | solution.py:357
  1222.3 462.0 %all-gather.55.cloned.1.call-start = ((), (), s32[]{:S(2)}) async-start(), calls=%async_computation.37 | async-start | bytes 1216512 | tf_op jit(solution)/shard_map/while/body/eval_jaxpr/all_gather | solution.py:358
  1223.0 517.2 %all-gather.57.cloned.1.call-start = ((), (), s32[]{:S(2)}) async-start(), calls=%async_computation.38 | async-start | bytes 1216512 | tf_op jit(solution)/shard_map/while/body/eval_jaxpr/all_gather | solution.py:361
  1223.8 572.2 %all-gather.59.cloned.1.call-start = ((), (), s32[]{:S(2)}) async-start(), calls=%async_computation.39 | async-start | bytes 1216512 | tf_op jit(solution)/shard_map/while/body/eval_jaxpr/all_gather | solution.py:362
  1802.2 352.3 %all-gather.51.cloned.1.call-start = ((), (), s32[]{:S(2)}) async-start(), calls=%async_computation.35 | async-start | bytes 1216512 | tf_op jit(solution)/shard_map/while/body/eval_jaxpr/all_gather | solution.py:356
  1802.8 407.5 %all-gather.53.cloned.1.call-start = ((), (), s32[]{:S(2)}) async-start(), calls=%async_computation.36 | async-start | bytes 1216512 | tf_op jit(solution)/shard_map/while/body/eval_jaxpr/all_gather | solution.py:357
  1803.3 462.8 %all-gather.55.cloned.1.call-start = ((), (), s32[]{:S(2)}) async-start(), calls=%async_computation.37 | async-start | bytes 1216512 | tf_op jit(solution)/shard_map/while/body/eval_jaxpr/all_gather | solution.py:358
  1804.1 517.8 %all-gather.57.cloned.1.call-start = ((), (), s32[]{:S(2)}) async-start(), calls=%async_computation.38 | async-start | bytes 1216512 | tf_op jit(solution)/shard_map/while/body/eval_jaxpr/all_gather | solution.py:361
  1804.7 573.1 %all-gather.59.cloned.1.call-start = ((), (), s32[]{:S(2)}) async-start(), calls=%async_computation.39 | async-start | bytes 1216512 | tf_op jit(solution)/shard_map/while/body/eval_jaxpr/all_gather | solution.py:362
  2382.2 415.4 %reduce-scatter.17.cloned.1.call-start = ((), (), s32[]{:S(2)}) async-start(), calls=%async_computation.13 | async-start | bytes 2433024 | tf_op jit(solution)/shard_map/reduce_scatter | solution.py:391
  2382.9 518.4 %reduce-scatter.19.cloned.1.call-start = ((), (), s32[]{:S(2)}) async-start(), calls=%async_computation.14 | async-start | bytes 2433024 | tf_op jit(solution)/shard_map/reduce_scatter | solution.py:392
  2383.7 622.3 %reduce-scatter.21.cloned.1.call-start = ((), (), s32[]{:S(2)}) async-start(), calls=%async_computation.15 | async-start | bytes 2433024 | tf_op jit(solution)/shard_map/reduce_scatter | solution.py:393
  2384.4 725.3 %reduce-scatter.23.cloned.1.call-start = ((), (), s32[]{:S(2)}) async-start(), calls=%async_computation.16 | async-start | bytes 2433024 | tf_op jit(solution)/shard_map/reduce_scatter | solution.py:394
  2385.0 829.3 %reduce-scatter.25.cloned.1.call-start = ((), (), s32[]{:S(2)}) async-start(), calls=%async_computation.17 | async-start | bytes 2433024 | tf_op jit(solution)/shard_map/reduce_scatter | solution.py:395
  2385.6 969.7 %reduce-scatter.27.cloned.1.call-start = ((), (), s32[]{:S(2)}) async-start(), calls=%async_computation.18 | async-start | bytes 9732096 | tf_op jit(solution)/shard_map/reduce_scatter | solution.py:396
  2386.2 1111.3 %reduce-scatter.29.cloned.1.call-start = ((), (), s32[]{:S(2)}) async-start(), calls=%async_computation.19 | async-start | bytes 9732096 | tf_op jit(solution)/shard_map/reduce_scatter | solution.py:397
  (241 other events, 10331.9 us)
Sparse Core Ops, SparseCore 0:
  23.8 56.8 all-gather.20
  139.5 52.9 all-gather.24
  195.2 52.9 all-gather.28
  251.0 52.9 all-gather.26
  306.7 52.9 all-gather.30
  474.4 62.5 all-gather.38
  539.8 62.4 all-gather.36
  612.3 53.0 all-gather.20
  835.5 52.9 all-gather.26
  947.0 52.9 all-gather.32
  1058.7 62.5 all-gather.38
  1124.0 62.4 all-gather.36
  1221.3 62.9 all-gather.42
  1287.2 62.2 all-gather.44
  1519.7 52.9 all-gather.50
  1687.2 52.9 all-gather.56
  1743.0 52.9 all-gather.58
  1802.4 63.4 all-gather.42
  1868.8 62.4 all-gather.44
  1989.8 52.9 all-gather.48
  2101.5 52.9 all-gather.50
  2157.2 52.9 all-gather.52
  2268.9 52.9 all-gather.56
  2324.8 52.9 all-gather.58
  (16 shorter events, 846.1 us)
Sparse Core Ops, SparseCore 1:
  2386.8 97.7 reduce-scatter.10
  2491.1 98.0 reduce-scatter.12
  2594.9 97.9 reduce-scatter.14
  2699.5 97.9 reduce-scatter.16
  2803.4 97.9 reduce-scatter.18
  2908.1 97.9 reduce-scatter.20
  3011.7 97.9 reduce-scatter.22
  3116.3 97.9 reduce-scatter.24
  3220.6 134.6 reduce-scatter.26
  3362.8 134.6 reduce-scatter.28
where the time goes:
time: 3510 us
  waiting for transfers between devices  2860 us (81%)
  matrix products  238 us (7%)
  blocking collectives  203 us (6%)
  local copies, waits for them, and re-layouts  99.7 us (3%)
  other arithmetic  59.6 us (2%)
    while x4, blocking collectives  164 us
    reduce_scatter x1, waiting for transfers between devices, body(): lax.psum_scatter(running[9], ('dp', 'fsdp'), scatter_dimension=0, tiled=T...  142 us
    reduce_scatter x1, waiting for transfers between devices, body(): lax.psum_scatter(running[8], ('dp', 'fsdp'), scatter_dimension=0, tiled=T...  141 us
    all_gather x2, waiting for transfers between devices, run_forward(): lax.all_gather(ff_in, ('dp', 'fsdp'), axis=0, tiled=True)  120 us
    all_gather x2, waiting for transfers between devices, run_forward(): lax.all_gather(ff_out, ('dp', 'fsdp'), axis=0, tiled=True)  112 us
    all_gather x2, waiting for transfers between devices, run_forward(): lax.all_gather(cross_query, ('dp', 'fsdp'), axis=0, tiled=True)  108 us
    all_gather x2, waiting for transfers between devices, run_forward(): lax.all_gather(cross_key, ('dp', 'fsdp'), axis=0, tiled=True)  108 us
    all_gather x2, waiting for transfers between devices, run_backward(): lax.all_gather(self_key, ('dp', 'fsdp'), axis=0, tiled=True)  106 us
  transfers between devices with their start and end apart: 50, of which 47 were waited for; matrix products, arithmetic and copies ran while one was open for 9% of the time, Pallas kernels for 0%

commit v1 on v0

v1 whole, which is shorter than its diff:
```python
import math

import jax
import jax.numpy as jnp
from jax import lax
from jax.sharding import PartitionSpec as P

HEADS = 12
BUCKETS = 32
MAX_DIST = 128


EPS = 1e-06
MASKED = -1e30
TOP_PRECISION = lax.Precision.HIGHEST


def bucket_onehot(length):
    half_count = BUCKETS // 2
    positions = jnp.arange(length, dtype=jnp.int32)
    distance = jnp.maximum(positions[:, None] - positions[None, :], 0)
    farther = jnp.zeros_like(distance)
    for level in range(1, half_count):
        border = int(math.ceil(half_count * (MAX_DIST / half_count) ** (level / half_count)))
        farther = farther + (distance >= border).astype(jnp.int32)
    bucket = jnp.where(distance < half_count, distance, half_count + farther)
    return (bucket[None] == jnp.arange(BUCKETS, dtype=jnp.int32)[:, None, None]).astype(jnp.float32)


def normalize(vector, gain_row):
    return vector * lax.rsqrt(jnp.mean(vector * vector, axis=-1, keepdims=True) + EPS) * gain_row


def project(operand, weight):
    return jnp.dot(operand, weight, preferred_element_type=jnp.float32)


def project_back(operand, weight):
    return lax.dot_general(
        operand, weight, (((1,), (1,)), ((), ())), preferred_element_type=jnp.float32
    )


def weight_grad(inputs_rows, grad_rows):
    return lax.dot_general(
        inputs_rows, grad_rows, (((0,), (0,)), ((), ())), preferred_element_type=jnp.float32
    )


def split_heads(matrix):
    return matrix.reshape(matrix.shape[:-1] + (HEADS, matrix.shape[-1] // HEADS))


def head_scores(queries, key_rows):
    return jnp.einsum(
        "gqhe,gkhe->ghqk",
        split_heads(queries),
        split_heads(key_rows),
        preferred_element_type=jnp.float32,
    )


def attend_forward(queries, key_rows, values, relative_position_bias, allowed):
    scores = jnp.where(allowed, head_scores(queries, key_rows) + relative_position_bias, MASKED)
    largest = jnp.max(scores, axis=-1, keepdims=True)
    exponent = jnp.exp(scores - largest)
    row_totals = jnp.sum(exponent, axis=-1, keepdims=True)
    attention_weights = exponent / row_totals
    context = jnp.einsum(
        "ghqk,gkhe->gqhe",
        attention_weights.astype(jnp.bfloat16),
        split_heads(values),
        preferred_element_type=jnp.float32,
    )
    return (context.reshape(queries.shape).astype(jnp.bfloat16), attention_weights)


def attend_backward(queries, key_rows, values, attention_weights, grad_context):
    grad_heads = split_heads(grad_context)
    grad_values = jnp.einsum(
        "ghqk,gqhe->gkhe",
        attention_weights.astype(jnp.bfloat16),
        grad_heads,
        preferred_element_type=jnp.float32,
    )
    grad_weights = jnp.einsum(
        "gqhe,gkhe->ghqk", grad_heads, split_heads(values), preferred_element_type=jnp.float32
    )
    score_gradient = attention_weights * (
        grad_weights - jnp.sum(grad_weights * attention_weights, axis=-1, keepdims=True)
    )
    rounded = score_gradient.astype(jnp.bfloat16)
    grad_queries = jnp.einsum(
        "ghqk,gkhe->gqhe", rounded, split_heads(key_rows), preferred_element_type=jnp.float32
    )
    grad_keys = jnp.einsum(
        "ghqk,gqhe->gkhe", rounded, split_heads(queries), preferred_element_type=jnp.float32
    )
    return (
        grad_queries.reshape(queries.shape).astype(jnp.bfloat16),
        grad_keys.reshape(key_rows.shape).astype(jnp.bfloat16),
        grad_values.reshape(values.shape).astype(jnp.bfloat16),
        score_gradient,
    )


AXES = ("dp", "fsdp")


def rows_of(matrix):
    return matrix.reshape(-1, matrix.shape[-1])


def gather_all(shards):
    width = shards[0].shape[1]
    blocks = []
    for shard in shards:
        if shard.ndim == 1:
            continue
        blocks.append(shard.reshape(-1, width) if shard.shape[1] != width else shard)
    packed = lax.all_gather(jnp.concatenate(blocks, axis=0), AXES, axis=0)
    whole, at = [], 0
    devices = packed.shape[0]
    for shard, block in zip(shards, blocks):
        part = packed[:, at : at + block.shape[0]]
        at += block.shape[0]
        whole.append(part.reshape(devices * shard.shape[0], shard.shape[1]))
    gains = jnp.stack(shards[len(blocks) :])
    gains = lax.all_gather(gains, AXES, axis=1, tiled=True)
    return whole, [gains[k] for k in range(gains.shape[0])]


def scatter_all(grads, shards):
    width = shards[0].shape[1]
    devices = lax.axis_size(AXES)
    blocks = [grad.astype(jnp.bfloat16).reshape(devices, -1, width) for grad in grads]
    summed = lax.psum_scatter(
        jnp.concatenate(blocks, axis=1), AXES, scatter_dimension=0, tiled=False
    ).astype(jnp.float32)
    pieces, at = [], 0
    for block, shard in zip(blocks, shards):
        pieces.append(summed[at : at + block.shape[1]].reshape(shard.shape))
        at += block.shape[1]
    return pieces


def body(decoder_in, memory, out_grad, lengths, *params):
    shards, bucket_bias_table = params[:13], params[13]
    matrices, gains = gather_all(shards)
    (
        self_query,
        self_key,
        self_value,
        self_out,
        cross_query,
        cross_key,
        cross_value,
        cross_out,
        ff_in,
        ff_out,
    ) = matrices
    norm_self, norm_cross, norm_ff = [gain.astype(jnp.float32) for gain in gains]
    micro, seqs, seq_length, width = decoder_in.shape
    groups = micro * seqs
    memory_bf = memory.reshape(groups, memory.shape[2], width)
    grad_bf = out_grad.reshape(groups, seq_length, width)
    group_lengths = lengths.reshape(groups)
    bucket_indicator = bucket_onehot(seq_length)
    relative_position_bias = jnp.einsum(
        "fsn,fe->esn",
        bucket_indicator,
        bucket_bias_table.astype(jnp.float32),
        precision=TOP_PRECISION,
    )
    positions = jnp.arange(seq_length, dtype=jnp.int32)
    causal = positions[:, None] >= positions[None, :]
    present = positions[None, :] < group_lengths[:, None]
    valid_rows = present[:, :, None].astype(jnp.float32)
    allowed = causal[None, None] & present[:, None, None, :]

    def grad_of(inputs, upstream):
        return weight_grad(rows_of(inputs), rows_of(upstream))

    decoded = decoder_in.reshape(groups, seq_length, width).astype(jnp.float32)
    normed = normalize(decoded, norm_self).astype(jnp.bfloat16)
    queries = project(normed, self_query).astype(jnp.bfloat16)
    key_rows = project(normed, self_key).astype(jnp.bfloat16)
    values = project(normed, self_value).astype(jnp.bfloat16)
    context, self_weights = attend_forward(
        queries, key_rows, values, relative_position_bias, allowed
    )
    after_self = decoded + project(context, self_out)
    normed_cross = normalize(after_self, norm_cross).astype(jnp.bfloat16)
    cross_queries = project(normed_cross, cross_query).astype(jnp.bfloat16)
    memory_keys = project(memory_bf, cross_key).astype(jnp.bfloat16)
    memory_values = project(memory_bf, cross_value).astype(jnp.bfloat16)
    cross_context, cross_weights = attend_forward(
        cross_queries, memory_keys, memory_values, 0.0, True
    )
    after_cross = after_self + project(cross_context, cross_out)
    normed_ff = normalize(after_cross, norm_ff).astype(jnp.bfloat16)
    hidden = project(normed_ff, ff_in)
    activated = jax.nn.gelu(hidden, approximate=True).astype(jnp.bfloat16)
    after_ff = after_cross + project(activated, ff_out)
    layer_out = (after_ff * valid_rows).astype(jnp.bfloat16)

    def back(operand, weight):
        return lax.dot_general(
            operand, weight, (((2,), (1,)), ((), ())), preferred_element_type=jnp.float32
        )

    grad_after = grad_bf.astype(jnp.float32) * valid_rows
    grad_branch = grad_after.astype(jnp.bfloat16)
    grad_ff_out = grad_of(activated, grad_branch)
    gelu_pull = jax.vjp(lambda pre_act: jax.nn.gelu(pre_act, approximate=True), hidden)[1]
    grad_hidden = gelu_pull(back(grad_branch, ff_out))[0].astype(jnp.bfloat16)
    grad_ff_in = grad_of(normed_ff, grad_hidden)
    norm_pull = jax.vjp(normalize, after_cross, norm_ff)[1]
    grad_rows, grad_norm_ff = norm_pull(back(grad_hidden, ff_in))
    grad_after = grad_after + grad_rows
    grad_branch = grad_after.astype(jnp.bfloat16)
    grad_cross_out = grad_of(cross_context, grad_branch)
    grad_context = back(grad_branch, cross_out).astype(jnp.bfloat16)
    grad_cross_rows, grad_memory_keys, grad_memory_values, unused = attend_backward(
        cross_queries, memory_keys, memory_values, cross_weights, grad_context
    )
    grad_cross_query = grad_of(normed_cross, grad_cross_rows)
    grad_cross_key = grad_of(memory_bf, grad_memory_keys)
    grad_cross_value = grad_of(memory_bf, grad_memory_values)
    grad_memory = back(grad_memory_keys, cross_key) + back(grad_memory_values, cross_value)
    norm_pull = jax.vjp(normalize, after_self, norm_cross)[1]
    grad_rows, grad_norm_cross = norm_pull(back(grad_cross_rows, cross_query))
    grad_after = grad_after + grad_rows
    grad_branch = grad_after.astype(jnp.bfloat16)
    grad_self_out = grad_of(context, grad_branch)
    grad_context = back(grad_branch, self_out).astype(jnp.bfloat16)
    grad_queries, grad_key_rows, grad_values, score_gradient = attend_backward(
        queries, key_rows, values, self_weights, grad_context
    )
    grad_self_query = grad_of(normed, grad_queries)
    grad_self_key = grad_of(normed, grad_key_rows)
    grad_self_value = grad_of(normed, grad_values)
    grad_normed = (
        back(grad_queries, self_query) + back(grad_key_rows, self_key) + back(grad_values, self_value)
    )
    norm_pull = jax.vjp(normalize, decoded, norm_self)[1]
    grad_rows, grad_norm_self = norm_pull(grad_normed)
    grad_input = grad_after + grad_rows
    bias_grad = jnp.einsum(
        "fgd,ogd->fo", bucket_indicator, jnp.sum(score_gradient, axis=0), precision=TOP_PRECISION
    )
    pieces = scatter_all(
        (
            grad_self_query,
            grad_self_key,
            grad_self_value,
            grad_self_out,
            grad_cross_query,
            grad_cross_key,
            grad_cross_value,
            grad_cross_out,
            grad_ff_in,
            grad_ff_out,
        ),
        shards[:10],
    )
    small = lax.psum(
        jnp.concatenate([grad_norm_self, grad_norm_cross, grad_norm_ff, bias_grad.reshape(-1)]),
        AXES,
    )
    mine = shards[10].shape[0]
    at = lax.axis_index(AXES) * mine
    gains_out = [
        lax.dynamic_slice_in_dim(small[k * width : (k + 1) * width], at, mine) for k in range(3)
    ]
    return (
        layer_out.reshape(decoder_in.shape),
        grad_input.reshape(decoder_in.shape),
        grad_memory.reshape(memory.shape),
        *pieces,
        *gains_out,
        small[3 * width :].reshape(bucket_bias_table.shape),
    )


def solution(mesh):
    return jax.shard_map(
        body,
        mesh=mesh,
        in_specs=(
            P(None, ("dp", "fsdp"), None, None),
            P(None, ("dp", "fsdp"), None, None),
            P(None, ("dp", "fsdp"), None, None),
            P(None, ("dp", "fsdp")),
            P(("dp", "fsdp"), None),
            P(("dp", "fsdp"), None),
            P(("dp", "fsdp"), None),
            P(("dp", "fsdp"), None),
            P(("dp", "fsdp"), None),
            P(("dp", "fsdp"), None),
            P(("dp", "fsdp"), None),
            P(("dp", "fsdp"), None),
            P(("dp", "fsdp"), None),
            P(("dp", "fsdp"), None),
            P(("dp", "fsdp")),
            P(("dp", "fsdp")),
            P(("dp", "fsdp")),
            P(),
        ),
        out_specs=(
            P(None, ("dp", "fsdp"), None, None),
            P(None, ("dp", "fsdp"), None, None),
            P(None, ("dp", "fsdp"), None, None),
            P(("dp", "fsdp"), None),
            P(("dp", "fsdp"), None),
            P(("dp", "fsdp"), None),
            P(("dp", "fsdp"), None),
            P(("dp", "fsdp"), None),
            P(("dp", "fsdp"), None),
            P(("dp", "fsdp"), None),
            P(("dp", "fsdp"), None),
            P(("dp", "fsdp"), None),
            P(("dp", "fsdp"), None),
            P(("dp", "fsdp")),
            P(("dp", "fsdp")),
            P(("dp", "fsdp")),
            P(),
        ),
        check_vma=False,
    )
```

time: 3510 us -> 529 us (0.15)
  waiting for transfers between devices: 2860 us -> 193 us
  matrix products: 238 us -> 117 us
  blocking collectives: 203 us -> 82.2 us
  other arithmetic: 59.6 us -> 16.5 us
    all_gather x40 -> x1, waiting for transfers between devices: 1760 us -> 61.4 us  [gather_all(): packed = lax.all_gather(jnp.concatenate(blocks, axis=0), AXES, axis=0)]
    reduce_scatter x10 -> x1, waiting for transfers between devices: 1070 us -> 131 us  [scatter_all(): lax.psum_scatter(jnp.concatenate(blocks, axis=1), AXES, scatter_dimension...]
    while x4 -> x0, blocking collectives: 164 us -> none
    dot_general x50 -> x21, matrix products: 116 us -> 59.5 us  [the longest x10 24.4 us: back(): lax.dot_general(operand, weight, (((2,), (1,)), ((), ())), preferred_elem...]
    while x440 -> x0, local copies, waits for them, and re-layouts: 44.9 us -> none
    all_gather x0 -> x1, blocking collectives: none -> 43.5 us  [gather_all(): gains = lax.all_gather(gains, AXES, axis=1, tiled=True)]
    unnamed x1 -> x0, blocking collectives: 39.5 us -> none
    psum x0 -> x1, blocking collectives: none -> 38.7 us  [body(): lax.psum(jnp.concatenate([grad_norm_self, grad_norm_cross, grad_norm_ff,...]
  transfers between devices with their start and end apart: 50 -> 2, of which waited for: 47 -> 2; matrix products, arithmetic and copies ran while one was open for 9% -> 11% of each run, Pallas kernels for 0% -> 0%
where the time goes in v1:
time: 529 us; the launch traced here: 519 us
  waiting for transfers between devices  193 us (36%)
  matrix products  117 us (22%)
  local copies, waits for them, and re-layouts  95.1 us (18%)
  blocking collectives  82.2 us (16%)
  other arithmetic  16.5 us (3%)
  between operations  15.4 us (3%)
    reduce_scatter x1, waiting for transfers between devices, scatter_all(): lax.psum_scatter(jnp.concatenate(blocks, axis=1), AXES, scatter_dimension...  131 us
    all_gather x1, waiting for transfers between devices, gather_all(): packed = lax.all_gather(jnp.concatenate(blocks, axis=0), AXES, axis=0)  61.4 us
    all_gather x1, blocking collectives, gather_all(): gains = lax.all_gather(gains, AXES, axis=1, tiled=True)  43.5 us
    psum x1, blocking collectives, body(): lax.psum(jnp.concatenate([grad_norm_self, grad_norm_cross, grad_norm_ff,...  38.7 us
    unnamed x174, local copies, waits for them, and re-layouts  26.4 us
    dot_general x10, matrix products, project(): return jnp.dot(operand, weight, preferred_element_type=jnp.float32)  24.7 us
    dot_general x10, matrix products, back(): lax.dot_general(operand, weight, (((2,), (1,)), ((), ())), preferred_elem...  24.4 us
    dot_general x10, matrix products, weight_grad(): lax.dot_general(inputs_rows, grad_rows, (((0,), (0,)), ((), ())), preferr...  19.3 us
  transfers between devices with their start and end apart: 2, of which 2 were waited for; matrix products, arithmetic and copies ran while one was open for 11% of the time, Pallas kernels for 0%

profile of v1, /device:TPU:0, one launch (start us, length us, event | category | flops | bytes accessed | tf_op | source)
XLA Modules:
  0.0 519.3 jit_solution(13401734092992785009)
XLA Ops:
  16.4 43.5 %all-gather.1 = bf16[32,24,3]{1,2,0:T(4,128)(2,1)S(1)} all-gather(bf16[1,24,3]{1,2,0:T(4,128)(2,1)S(1)} %maximum_bitcast_fusion), channel_id=1, replica_groups=mesh['dp'=8,'fsdp'=4] {'dp','fsdp'}, dimensions={0}, use_global_device_ids=true | all-gather | bytes 4752 | tf_op jit(solution)/shard_map/all_gather | solution.py:129
  62.2 11.5 %copy.135 = pred[32,256,256]{2,0,1:T(32,128)(4,1)S(1)} copy(pred[32,256,256]{1,0,2:T(32,128)(4,1)S(1)} %iota_compare_fusion) | data formatting | bytes 4194304 | tf_op jit(solution)/shard_map/eq | solution.py:27
  73.6 3.1 convolution_bitcast_fusion
  76.8 5.1 copy.136
  82.5 61.4 %all-gather.4.cloned.1.call-done = bf16[12288,768]{1,0:T(8,128)(2,1)} async-done(((bf16[384,768]{1,0:T(8,128)(2,1)}), bf16[12288,768]{1,0:T(8,128)(2,1)}) %all-gather.4.cloned.1.call-update) | async-done | bytes 18874384 | tf_op jit(solution)/shard_map/all_gather | solution.py:121
  143.8 6.8 %fusion.106 = (bf16[32,24,768]{2,1,0:T(8,128)(2,1)}, bf16[32,24,768]{2,1,0:T(8,128)(2,1)}, bf16[32,24,768]{2,1,0:T(8,128)(2,1)}, bf16[32,24,768]{2,1,0:T(8,128)(...) fusion(bf16[32,384,768]{2,1,0:T(8,128)(2,1)} %bitcast.295), kind=kLoop, calls=%fused_computation.192 | loop fusion | bytes 18874368 | tf_op jit(solution)/shard_map/slice | solution.py:125
  150.7 8.5 %fusion.105 = (bf16[32,96,768]{2,1,0:T(8,128)(2,1)}, bf16[32,96,768]{2,1,0:T(8,128)(2,1)}) fusion(bf16[32,384,768]{2,1,0:T(8,128)(2,1)} %bitcast.296), kind=kLoop, calls=%fused_computation.191 | loop fusion | bytes 18874368 | tf_op jit(solution)/shard_map/slice | solution.py:125
  159.1 8.6 %reshape.483 = bf16[768,3072,1]{1,0,2:T(8,128)(2,1)} reshape(bf16[32,96,768]{2,1,0:T(8,128)(2,1)} %get-tuple-element.77) | data formatting | bytes 9437184 | tf_op jit(solution)/shard_map/reshape | solution.py:127
  183.2 6.9 %fusion.108 = (f32[2,12,256]{2,1,0:T(8,128)S(1)}, f32[2,12,256,256]{2,3,1,0:T(8,128)}) fusion(f32[12,256,256]{1,2,0:T(8,128)} %copy.136, pred[2,256,256]{1,2,0:T(8,128)(4,1)S(1)} %broadcast_and_fusion, bf16[2,256,12,64]{1,3,2,0:T(8,128)(2,1)S(1)} %bitcast.329, bf16[2,256,12,64]{1,3,2,0:T(8,128)(2,1)S(1)} %bitcast.327), kind=kOutput, calls=%fused_computation.194 | convolution fusion | flops 207618304 | bytes 11165696 | tf_op jit(solution)/shard_map/sub | solution.py:66
  190.1 3.8 fusion.39
  198.6 4.0 fusion.109
  209.4 5.2 bitcast_convert_fusion
  214.6 7.9 %fusion.8 = bf16[2,256,3072]{2,1,0:T(8,128)(2,1)S(1)} fusion(f32[2,256,3072]{2,1,0:T(8,128)S(1)} %fusion.89, bf16[3072,768,1]{1,0,2:T(8,128)(2,1)S(1)} %bitcast.322, bf16[2,1,256,768]{3,2,1,0:T(8,128)(2,1)S(1)} %copy-done.36, f32[2,256]{1,0:T(2,128)S(1)} %get-tuple-element.100), kind=kOutput, calls=%fused_computation.13 | convolution fusion | flops 2448556032 | bytes 14944256 | tf_op jit(solution)/shard_map/dot_general | solution.py:208
  222.5 3.4 multiply_reduce_fusion.2
  225.9 4.6 bitcast_convert_fusion.1
  234.1 3.5 convolution_convert_fusion.12
  250.7 4.8 fusion.42
  255.5 6.5 %multiply_reduce_fusion = (f32[2,12,256]{2,1,0:T(8,128)S(1)}, f32[2,12,256,256]{2,3,1,0:T(8,128)}) fusion(f32[2,12,256,256]{2,3,1,0:T(8,128)} %get-tuple-element.103, f32[2,12,256]{2,1,0:T(8,128)S(1)} %copy-done.51, bf16[2,256,12,64]{1,3,2,0:T(8,128)(2,1)S(1)} %bitcast.361, bf16[2,256,12,64]{1,3,2,0:T(8,128)(2,1)S(1)} %bitcast.357), kind=kOutput, calls=%fused_computation.15 | convolution fusion | flops 206039040 | bytes 14204928 | tf_op jit(solution)/shard_map/gqhe,gkhe->ghqk/dot_general | solution.py:86
  262.1 8.6 %fusion.15 = (f32[12,256,256]{1,2,0:T(8,128)}, bf16[2,12,256,256]{2,3,1,0:T(8,128)(2,1)S(1)}) fusion(f32[2,12,256,256]{2,3,1,0:T(8,128)} %get-tuple-element.115, f32[2,12,256]{2,1,0:T(8,128)S(1)} %get-tuple-element.114, f32[2,12,256,256]{2,3,1,0:T(8,128)} %get-tuple-element.103, f32[2,12,256]{2,1,0:T(8,128)S(1)} %copy-done.51), kind=kLoop, calls=%fused_computation.29 | loop fusion | flops 7077888 | bytes 18923520 | tf_op jit(solution)/shard_map/reduce_sum | solution.py:250
  274.2 8.5 %reshape.461 = bf16[32,96,768]{2,1,0:T(8,128)(2,1)} reshape(bf16[768,3072]{1,0:T(8,128)(2,1)} %bitcast_convert_fusion.1) | data formatting | bytes 9437184 | tf_op jit(solution)/shard_map/reshape | solution.py:136
  303.3 7.9 %fusion.47 = f32[32,12]{1,0:T(8,128)} fusion(f32[12,256,256]{1,2,0:T(8,128)} %get-tuple-element.87, s32[256,256]{0,1:T(8,128)} %copy-done.35), kind=kOutput, calls=%fused_computation.100 | convolution fusion | flops 304087040 | bytes 3409408 | tf_op jit(solution)/shard_map/fgd,ogd->fo/dot_general | solution.py:249
  320.2 38.7 %psum.7 = f32[2688]{0:T(1024)S(1)} all-reduce(f32[2688]{0:T(1024)} %pad_maximum_fusion), channel_id=1, replica_groups=mesh['dp'=8,'fsdp'=4] {'dp','fsdp'}, use_global_device_ids=true, to_apply=%region_17.18 | all-reduce | flops 2688 | bytes 21504 | tf_op jit(solution)/shard_map/psum | solution.py:267
  368.4 8.9 %fusion.45 = bf16[2,1,256,768]{3,2,1,0:T(8,128)(2,1)} fusion(f32[2,256,768]{2,1,0:T(8,128)S(1)} %copy-done.4, bf16[3072,768,1]{1,0,2:T(8,128)(2,1)} %bitcast.319, f32[2,256]{1,0:T(2,128)S(1)} %copy-done.58, f32[2,256,3072]{2,1,0:T(8,128)} %copy-done.10), kind=kOutput, calls=%fused_computation.93 | convolution fusion | flops 2431254528 | bytes 13371392 | tf_op jit(solution)/shard_map/dot_general | solution.py:35
  377.2 131.2 %reduce-scatter.2.cloned.1.call-done = bf16[1,384,768]{2,1,0:T(8,128)(2,1)} async-done(((bf16[32,384,768]{2,1,0:T(8,128)(2,1)}), bf16[1,384,768]{2,1,0:T(8,128)(2,1)}) %reduce-scatter.2.cloned.1.call-update) | async-done | bytes 589840 | tf_op jit(solution)/shard_map/reduce_scatter | solution.py:137
  (256 shorter events, 101.0 us)
Async XLA Ops:
  7.2 160.6 %copy-start = (bf16[2,1,128,768]{3,2,1,0:T(8,128)(2,1)S(1)}, bf16[2,1,128,768]{3,2,1,0:T(8,128)(2,1)}, u32[]{:S(2)}) copy-start(bf16[2,1,128,768]{3,2,1,0:T(8,128)(2,1)} %param.19) | copy-start | bytes 1179652
  7.2 9.1 %copy-start.64 = (bf16[24]{0:T(256)(128)(2,1)S(1)}, bf16[24]{0:T(256)(128)(2,1)}, u32[]{:S(2)}) copy-start(bf16[24]{0:T(256)(128)(2,1)} %param.34) | copy-start | bytes 148
  7.2 9.1 %copy-start.65 = (bf16[24]{0:T(256)(128)(2,1)S(1)}, bf16[24]{0:T(256)(128)(2,1)}, u32[]{:S(2)}) copy-start(bf16[24]{0:T(256)(128)(2,1)} %param.33) | copy-start | bytes 148
  7.2 9.1 %copy-start.66 = (bf16[24]{0:T(256)(128)(2,1)S(1)}, bf16[24]{0:T(256)(128)(2,1)}, u32[]{:S(2)}) copy-start(bf16[24]{0:T(256)(128)(2,1)} %param.32) | copy-start | bytes 148
  7.2 136.6 %all-gather.4.cloned.1.call-start = ((), (), s32[]{:S(2)}) async-start(), calls=%async_computation.2 | async-start | bytes 19464192 | tf_op jit(solution)/shard_map/all_gather | solution.py:121
  16.3 492.1 %reduce-scatter.2.cloned.1.call-start = ((), (), s32[]{:S(2)}) async-start(), calls=%async_computation.1 | async-start | bytes 19464192 | tf_op jit(solution)/shard_map/reduce_scatter | solution.py:137
  62.1 11.5 %copy-start.63 = (bf16[32,12]{0,1:T(8,128)(2,1)S(1)}, bf16[32,12]{0,1:T(8,128)(2,1)}, u32[]{:S(2)}) copy-start(bf16[32,12]{0,1:T(8,128)(2,1)} %param.35) | copy-start | bytes 2308
  76.8 5.5 %copy-start.67 = (s32[2,1]{0,1:T(1,128)S(1)}, s32[2,1]{0,1:T(1,128)}, u32[]{:S(2)}) copy-start(s32[2,1]{0,1:T(1,128)} %param.21) | copy-start | bytes 28
  81.9 234.0 %copy-start.48 = (f32[768]{0:T(1024)}, f32[768]{0:T(1024)S(1)}, u32[]{:S(2)}) copy-start(f32[768]{0:T(1024)S(1)} %get-tuple-element.76) | copy-start | bytes 9220
  82.2 68.5 %copy-start.52 = (f32[2,256]{1,0:T(2,128)}, f32[2,256]{1,0:T(2,128)S(1)}, u32[]{:S(2)}) copy-start(f32[2,256]{1,0:T(2,128)S(1)} %fusion.22) | copy-start | bytes 6148
  82.3 132.3 %copy-start.56 = (f32[2,256]{1,0:T(2,128)}, f32[2,256]{1,0:T(2,128)S(1)}, u32[]{:S(2)}) copy-start(f32[2,256]{1,0:T(2,128)S(1)} %get-tuple-element.100) | copy-start | bytes 6148
  82.3 96.8 %copy-start.53 = (f32[2,256]{1,0:T(2,128)}, f32[2,256]{1,0:T(2,128)S(1)}, u32[]{:S(2)}) copy-start(f32[2,256]{1,0:T(2,128)S(1)} %fusion.94) | copy-start | bytes 6148
  150.7 19.8 %copy-start.12 = (bf16[32,24,768]{2,1,0:T(8,128)(2,1)}, bf16[32,24,768]{2,1,0:T(8,128)(2,1)S(1)}, u32[]{:S(2)}) copy-start(bf16[32,24,768]{2,1,0:T(8,128)(2,1)S(1)} %get-tuple-element.82) | copy-start | bytes 3538948
  175.0 8.2 %copy-start.21 = (bf16[2,256,768]{1,2,0:T(8,128)(2,1)}, bf16[2,256,768]{1,2,0:T(8,128)(2,1)S(1)}, u32[]{:S(2)}) copy-start(bf16[2,256,768]{1,2,0:T(8,128)(2,1)S(1)} %copy.134) | copy-start | bytes 2359300
  194.9 10.3 %copy-start.1 = (f32[2,256,768]{2,1,0:T(8,128)}, f32[2,256,768]{2,1,0:T(8,128)S(1)}, u32[]{:S(2)}) copy-start(f32[2,256,768]{2,1,0:T(8,128)S(1)} %get-tuple-element.105) | copy-start | bytes 4718596
  198.6 7.5 %slice-start = ((s8[4718592]{0:T(1024)(128)(4,1)}), s8[524288]{0:T(1024)(128)(4,1)S(1)}, s32[]{:S(2)}) async-start(s8[4718592]{0:T(1024)(128)(4,1)} %bitcast.297), calls=%async_computation.3 | async-start | bytes 1048576
  206.1 24.4 %copy-start.3 = (f32[2,256,768]{2,1,0:T(8,128)}, f32[2,256,768]{2,1,0:T(8,128)S(1)}, u32[]{:S(2)}) copy-start(f32[2,256,768]{2,1,0:T(8,128)S(1)} %get-tuple-element.109) | copy-start | bytes 4718596
  206.3 8.3 %slice-start.6 = ((s8[4718592]{0:T(1024)(128)(4,1)}), s8[4194304]{0:T(1024)(128)(4,1)S(1)}, s32[]{:S(2)}) async-start(s8[4718592]{0:T(1024)(128)(4,1)} %bitcast.320), calls=%async_computation.9 | async-start | bytes 8388608
  209.4 5.2 %copy-start.10 = (f32[2,256,3072]{2,1,0:T(8,128)}, f32[2,256,3072]{2,1,0:T(8,128)S(1)}, u32[]{:S(2)}) copy-start(f32[2,256,3072]{2,1,0:T(8,128)S(1)} %fusion.89) | copy-start | bytes 18874372
  262.1 8.6 %copy-start.24 = (bf16[2,256,768]{1,2,0:T(8,128)(2,1)S(1)}, bf16[2,256,768]{1,2,0:T(8,128)(2,1)}, u32[]{:S(2)}) copy-start(bf16[2,256,768]{1,2,0:T(8,128)(2,1)} %copy.133) | copy-start | bytes 2359300
  274.2 8.5 %copy-start.25 = (bf16[2,12,64,128]{3,2,1,0:T(8,128)(2,1)S(1)}, bf16[2,12,64,128]{3,2,1,0:T(8,128)(2,1)}, u32[]{:S(2)}) copy-start(bf16[2,12,64,128]{3,2,1,0:T(8,128)(2,1)} %convolution_convert_fusion.12) | copy-start | bytes 1179652
  274.2 8.9 %copy-start.20 = (bf16[2,12,64,128]{3,2,1,0:T(8,128)(2,1)S(1)}, bf16[2,12,64,128]{3,2,1,0:T(8,128)(2,1)}, u32[]{:S(2)}) copy-start(bf16[2,12,64,128]{3,2,1,0:T(8,128)(2,1)} %convolution_convert_fusion.13) | copy-start | bytes 1179652
  289.3 9.0 %slice-start.2 = ((s8[4718592]{0:T(1024)(128)(4,1)}), s8[4194304]{0:T(1024)(128)(4,1)S(1)}, s32[]{:S(2)}) async-start(s8[4718592]{0:T(1024)(128)(4,1)} %bitcast.299), calls=%async_computation.5 | async-start | bytes 8388608
  295.5 5.3 %slice-start.4 = ((s8[4718592]{0:T(1024)(128)(4,1)}), s8[4194304]{0:T(1024)(128)(4,1)S(1)}, s32[]{:S(2)}) async-start(s8[4718592]{0:T(1024)(128)(4,1)} %bitcast.313), calls=%async_computation.7 | async-start | bytes 8388608
  (55 other events, 135.7 us)
Sparse Core Ops, SparseCore 0:
  16.4 127.3 all-gather.3
  303.4 204.9 reduce-scatter.1
